TPU v7x, 256 devices: a whole 4x4x8 slice. The times are simulated.
256 devices in a mesh: seq: 16 (over z, x_hi), head: 16 (over y, x_lo, core).
Axes of the slice: x: 4 (x_hi: 2, x_lo: 2; x = x_hi * 2 + x_lo), y: 4, z: 8, core: 2. Of those that a mesh axis runs over, the one named last changes fastest.
Arguments:
- q_latent: bfloat16 [2048, 1536], P('seq'), may hold values from -6 to 6
- kv_new: bfloat16 [2048, 576], P('seq'), may hold values from -6 to 6
- cache: bfloat16 [3072, 576], P('seq'), may hold values from -56 to 56
- latent_gain: float32 [512], replicated, may hold values from 0.1 to 1.9
- positions: int32 [2048], P('seq'), may hold values from 0 to 2047, as said below
- w_uq: bfloat16 [1536, 24576], P(None, 'head'), may hold values from -0.15625 to 0.15625
- w_uk: bfloat16 [128, 128, 512], P('head'), may hold values from -0.5 to 0.5
- w_uv: bfloat16 [128, 512, 128], P('head'), may hold values from -1 to 1
- w_out: bfloat16 [16384, 7168], P('head', 'seq'), may hold values from -0.1875 to 0.1875
Outputs:
- attended: bfloat16 [2048, 7168], P('seq', 'head')
Inputs may be any that keep to these rules, and one draw needn't show every extreme that they name: positions holds every number below 2048 once; each aligned block of 64 rows holds consecutive rising numbers starting at a multiple of 64.
All inputs are finite; a program needn't handle non-finite values.
Results may differ from a plain program's by a relative error of at most 0.025.
Values may be sent and summed in bfloat16 or wider, within the bound.
No kernel may reach another device: no remote copies, remote signals or barrier semaphores. Data moves between devices by JAX's collectives and lax.ppermute only.
A program may use at most 128 MiB of HBM per device.

v0:
```python
import functools
import math

import jax
import jax.numpy as jnp
from jax import lax
from jax.experimental import pallas as pl
from jax.experimental.pallas import tpu as pltpu
from jax.sharding import PartitionSpec as P

KV_RANK = 512
ROPE = 64
NOPE = 128
VDIM = 128
RUN = 64
PREFIX = 3072
WIDE = 640
CHUNK = 512
AXES = ("seq", "head")
BIG = -1e30
F32 = jnp.float32
BF16 = jnp.bfloat16


def place_of(i):
    s, h = divmod(i, 16)
    return s // 2, s % 2, h // 4, (h // 2) % 2, h % 2


def index_of(z, xh, y, xl, c):
    return (z * 2 + xh) * 16 + y * 4 + xl * 2 + c


def pairs(to):
    moves = [(i, to(*place_of(i))) for i in range(256)]
    return [(i, index_of(*place)) for i, place in moves if place]


def next_to(i, size):
    return (i + 1 if i % 2 else i - 1) % size


SWAP_CORE = pairs(lambda z, xh, y, xl, c: (z, xh, y, xl, 1 - c))
SWAP_XH = pairs(lambda z, xh, y, xl, c: (z, 1 - xh, y, xl, c))
SWAP_MIRROR = pairs(lambda z, xh, y, xl, c: (z, 1 - xh, y, 1 - xl, c))
SWAP_Z = (
    pairs(lambda z, xh, y, xl, c: (z ^ 1, xh, y, xl, c)),
    pairs(lambda z, xh, y, xl, c: (next_to(z, 8), xh, y, xl, c)),
)
SWAP_Y = (
    pairs(lambda z, xh, y, xl, c: (z, xh, y ^ 1, xl, c)),
    pairs(lambda z, xh, y, xl, c: (z, xh, next_to(y, 4), xl, c)),
    pairs(lambda z, xh, y, xl, c: (z, xh, y ^ 2, xl, c)),
)


SWAP_XL = pairs(lambda z, xh, y, xl, c: (z, xh, y, 1 - xl, c))
TO_PLACE = pairs(lambda z, xh, y, xl, c: (2 * y + xl, xh, z >> 1, z & 1, c))


def permute(x, perm):
    return lax.ppermute(x, AXES, perm)


def angles(place, width):
    index = jnp.arange(width // 2, dtype=F32)
    inv_freq = jnp.exp(index * (-2.0 * math.log(10000.0) / width))
    return place[:, None] * inv_freq[None, :]


def query_kernel(lat_ref, wq_ref, wk_ref, cos_ref, sin_ref, mask_ref, out_ref):
    scale = (NOPE + ROPE) ** (-0.5) * math.log2(math.e)
    query = jnp.dot(lat_ref[...], wq_ref[...], preferred_element_type=F32).astype(BF16)
    for i in range(2):
        part = query[:, i * 192 : (i + 1) * 192]
        absorbed = jnp.dot(part[:, :NOPE], wk_ref[i], preferred_element_type=F32)
        out_ref[i, :, :KV_RANK] = (absorbed * scale).astype(BF16)
        rope = part[:, NOPE:].astype(F32)
        swapped = jnp.concatenate([rope[:, ROPE // 2 :], rope[:, : ROPE // 2]], axis=1)
        rotated = rope * cos_ref[...] + swapped * sin_ref[...]
        out_ref[i, :, KV_RANK:] = jnp.concatenate(
            [(rotated * scale).astype(BF16), mask_ref[...]], axis=1
        )


def queries(lat, w_uq, w_uk, cosine, sine, mask):
    rows = lat.shape[0]
    heads = w_uk.shape[0]
    whole = lambda i: (0, 0)
    return pl.pallas_call(
        query_kernel,
        grid=(heads // 2,),
        in_specs=[
            pl.BlockSpec(lat.shape, whole),
            pl.BlockSpec((w_uq.shape[0], 384), lambda i: (0, i)),
            pl.BlockSpec((2, NOPE, KV_RANK), lambda i: (i, 0, 0)),
            pl.BlockSpec(cosine.shape, whole),
            pl.BlockSpec(sine.shape, whole),
            pl.BlockSpec(mask.shape, whole),
        ],
        out_specs=pl.BlockSpec((2, rows, WIDE), lambda i: (i, 0, 0)),
        out_shape=jax.ShapeDtypeStruct((heads, rows, WIDE), BF16),
        compiler_params=pltpu.CompilerParams(vmem_limit_bytes=32 * 2**20),
        cost_estimate=pl.CostEstimate(
            flops=rows * heads * (1536 * 192 + 128 * 512) // 4,
            bytes_accessed=2**20,
            transcendentals=0,
        ),
    )(lat, w_uq, w_uk, cosine, sine, mask)


def lanes(x, fill):
    width = x.shape[1]
    blocks = [x[:, at : min(at + 128, width)] for at in range(0, width, 128)]
    short = 128 - blocks[-1].shape[1]
    if short:
        rest = jnp.full((x.shape[0], short), fill, x.dtype)
        blocks[-1] = jnp.concatenate([blocks[-1], rest], axis=1)
    return blocks


def attend_kernel(stack, kind, *refs):
    q_ref, k_ref, wv_ref = refs[:3]
    refs = list(refs[3:])
    bias_ref = refs.pop(0) if kind == "first" else None
    before = [(refs.pop(0), refs.pop(0)) for _ in range(2)] if kind in ("own", "packed") else []
    top_ref = refs.pop()
    s_ref = refs.pop()
    out_ref = refs[0]
    heads, rows, _ = q_ref.shape
    count = k_ref.shape[0]
    groups = heads // stack
    many = stack * rows
    cuts = [(at, min(at + CHUNK, count)) for at in range(0, count, CHUNK)]
    nt = (((1,), (1,)), ((), ()))
    lane = lax.broadcasted_iota(jnp.int32, (rows, 128), 1)

    def score(group, slot, cut):
        start, end = cut
        q = q_ref[pl.ds(group * stack, stack)].reshape(many, WIDE)
        scores = lax.dot_general(q, k_ref[start:end, :], nt, preferred_element_type=F32)
        if bias_ref is not None and start == 0:
            bias = jnp.concatenate([bias_ref[...]] * stack, axis=0)
            scores = jnp.concatenate([scores[:, :128] + bias, scores[:, 128:]], axis=1)
        s_ref[slot, :, start:end] = scores
        return functools.reduce(jnp.maximum, lanes(scores, BIG))

    def finish(group, latent, lse, kept):
        for i in range(stack):
            part = slice(i * rows, (i + 1) * rows)
            head = group * stack + i
            at = head * VDIM
            at = pl.ds(at if isinstance(at, int) else pl.multiple_of(at, VDIM), VDIM)
            value = jnp.dot(latent[part], wv_ref[head], preferred_element_type=F32)
            level = lse[part]
            if before:
                values, levels = [value], [level]
                for value_ref, level_ref in before:
                    values.append(value_ref[:, at])
                    chosen = jnp.where(lane == head, level_ref[...], 0.0)
                    levels.append(jnp.sum(chosen, axis=1, keepdims=True))
                best = functools.reduce(jnp.maximum, levels)
                shares = [jnp.exp2(x - best) for x in levels]
                whole = functools.reduce(jnp.add, shares)
                value = functools.reduce(jnp.add, [v * w for v, w in zip(values, shares)])
                value = value / whole
                level = best + jnp.log2(whole)
            out_ref[:, at] = value.astype(out_ref.dtype)
            kept = jnp.where(lane % 8 == head, level, kept)
        return kept

    def turn(group, kept, more):
        slot, other = group % 2, (group + 1) % 2
        top = jnp.max(top_ref[...], axis=1, keepdims=True)
        total = jnp.zeros((many, 128), F32)
        accum = None
        tops = []
        for start, end in cuts:
            weights = jnp.exp2(s_ref[slot, :, start:end] - top)
            for block in lanes(weights, 0.0):
                total = total + block
            mixed = jnp.dot(
                weights.astype(BF16), k_ref[start:end, :KV_RANK], preferred_element_type=F32
            )
            accum = mixed if accum is None else accum + mixed
            if more:
                tops.append(score(group + 1, other, (start, end)))
        if more:
            top_ref[...] = functools.reduce(jnp.maximum, tops)
        total = jnp.sum(total, axis=1, keepdims=True)
        return finish(group, (accum / total).astype(BF16), top + jnp.log2(total), kept)

    top_ref[...] = functools.reduce(jnp.maximum, [score(0, 0, cut) for cut in cuts])
    kept = lax.fori_loop(
        0, groups - 1, lambda g, kept: turn(g, kept, True), jnp.zeros((rows, 128), F32)
    )
    kept = turn(groups - 1, kept, False)
    if kind != "packed":
        refs[1][...] = kept
        return
    high = kept.astype(BF16)
    rest = kept - high.astype(F32)
    mid = rest.astype(BF16)
    low = (rest - mid.astype(F32)).astype(BF16)
    out_ref[:, heads * VDIM :] = jnp.where(lane < 8, high, jnp.where(lane < 16, mid, low))


def attend(q, keys, w_uv, kind, bias=None, before=()):
    heads, rows, _ = q.shape
    count = keys.shape[0]
    stack = 2
    operands = [q, keys, w_uv]
    if bias is not None:
        operands.append(bias)
    for pair in before:
        operands += pair
    wide = heads * VDIM
    out_shape = [jax.ShapeDtypeStruct((rows, wide), F32), jax.ShapeDtypeStruct((rows, 128), F32)]
    if kind == "packed":
        out_shape = [jax.ShapeDtypeStruct((rows, wide + 128), BF16)]
    spec = pl.BlockSpec(memory_space=pltpu.VMEM)
    return pl.pallas_call(
        functools.partial(attend_kernel, stack, kind),
        in_specs=[spec] * len(operands),
        out_specs=[spec] * len(out_shape),
        out_shape=out_shape,
        scratch_shapes=[
            pltpu.VMEM((2, stack * rows, -(-count // 128) * 128), F32),
            pltpu.VMEM((stack * rows, 128), F32),
        ],
        compiler_params=pltpu.CompilerParams(vmem_limit_bytes=24 * 2**20),
        cost_estimate=pl.CostEstimate(
            flops=rows * heads * count * (WIDE + KV_RANK) // 8,
            bytes_accessed=2**19,
            transcendentals=0,
        ),
    )(*operands)


def prepare_kernel(kv_ref, cache_ref, gain_ref, cos_ref, sin_ref, run_ref, own_ref, keys_ref):
    core = lax.axis_index("head") % 2
    rows = kv_ref.shape[0]
    half = cache_ref.shape[0] // 2
    spare = WIDE - KV_RANK - ROPE
    latent = kv_ref[:, :KV_RANK].astype(F32)
    square = jnp.sum(latent * latent, axis=1, keepdims=True) / KV_RANK + 1e-06
    normed = latent / jnp.sqrt(square) * gain_ref[...]
    rope = kv_ref[:, KV_RANK:].astype(F32)
    swapped = jnp.concatenate([rope[:, ROPE // 2 :], rope[:, : ROPE // 2]], axis=1)
    rotated = rope * cos_ref[...] + swapped * sin_ref[...]
    slot = lax.broadcasted_iota(jnp.int32, (rows, spare), 1)
    one_hot = (run_ref[...] == slot).astype(F32)
    keys_ref[:rows, :KV_RANK] = normed.astype(BF16)
    keys_ref[:rows, KV_RANK:] = jnp.concatenate([rotated, one_hot], axis=1).astype(BF16)
    keys_ref[rows:, :KV_RANK] = cache_ref[:, :KV_RANK]
    keys_ref[rows:, KV_RANK:] = jnp.concatenate(
        [cache_ref[:, KV_RANK:], jnp.zeros((2 * half, spare), BF16)], axis=1
    )
    for i in range(2):

        @pl.when(core == i)
        def _():
            own_ref[:half] = keys_ref[rows + i * half : rows + (i + 1) * half]
            own_ref[half:] = keys_ref[i * RUN : (i + 1) * RUN]


def prepare(kv_new, cache, gain, cosine, sine, run):
    rows, old = kv_new.shape[0], cache.shape[0]
    spec = pl.BlockSpec(memory_space=pltpu.VMEM)
    return pl.pallas_call(
        prepare_kernel,
        in_specs=[spec] * 6,
        out_specs=[spec] * 2,
        out_shape=[
            jax.ShapeDtypeStruct(((rows + old) // 2, WIDE), BF16),
            jax.ShapeDtypeStruct((rows + old, WIDE), BF16),
        ],
        compiler_params=pltpu.CompilerParams(vmem_limit_bytes=16 * 2**20),
    )(kv_new, cache, gain, cosine, sine, run)


def tie(*arrays):
    return lax.optimization_barrier(arrays)


def step_z(a, b):
    return permute(b, SWAP_Z[0]), permute(a, SWAP_Z[1])


def both_cores(*pieces):
    mine = jnp.concatenate(pieces, axis=0)
    return mine, permute(mine, SWAP_CORE)


def turning(place):
    angle = angles(place.astype(F32), ROPE)
    cosine, sine = jnp.cos(angle), jnp.sin(angle)
    return jnp.concatenate([cosine, cosine], axis=1), jnp.concatenate([-sine, sine], axis=1)


def per_device(q_latent, kv_new, cache, latent_gain, positions, w_uq, w_uk, w_uv, w_out):
    rows = q_latent.shape[0]
    heads = w_uk.shape[0]
    head_index = lax.axis_index("head")
    seq_index = lax.axis_index("seq")
    core = head_index % 2
    x_hi = seq_index % 2
    spare = WIDE - KV_RANK - ROPE

    run = positions // RUN
    lane = jnp.arange(128)[None, :]
    marks = jnp.where(
        lane == 0, run[:, None], jnp.where(lane == 1, (positions % RUN)[:, None], 0)
    ).astype(BF16)
    other = permute(jnp.concatenate([q_latent, marks], axis=1), SWAP_MIRROR)

    cos_own, sin_own = turning(positions + PREFIX)
    own, keys_0 = prepare(
        kv_new, cache, latent_gain[None, :], cos_own, sin_own, run[:, None]
    )
    a_1, b_1 = step_z(own, own)
    mask = lambda r: jnp.where(jnp.arange(spare)[None, :] > r[:, None], BIG, 0.0).astype(BF16)
    q_own = queries(q_latent, w_uq, w_uk, cos_own, sin_own, mask(run))
    q_own, a_1, b_1 = tie(q_own, a_1, b_1)

    a_2, b_2 = step_z(a_1, b_1)
    mine_1, theirs_1 = both_cores(a_1, b_1)
    keys_1 = jnp.concatenate([keys_0, mine_1, theirs_1], axis=0)
    token = jnp.arange(rows)[:, None]
    hidden = (token // RUN == lane // RUN) & (lane % RUN > token % RUN)
    bias = jnp.where(hidden, BIG, 0.0).astype(F32)
    own_1 = attend(q_own, keys_1, w_uv, "first", bias=bias)
    own_1, a_2, b_2, other = tie(own_1, a_2, b_2, other)

    a_3, b_3 = step_z(a_2, b_2)
    mine_2, theirs_2 = both_cores(a_2, b_2)
    w_half = w_out.shape[0] // 2
    w_sent, other = tie(w_out[:w_half], other)
    w_first = permute(w_sent, SWAP_XH)
    other_marks = other[:, 1536:1538].astype(jnp.int32)
    other_run = other_marks[:, 0]
    cos_other, sin_other = turning(other_run * RUN + other_marks[:, 1] + PREFIX)
    q_other = queries(
        other[:, :1536], w_uq, w_uk, cos_other, sin_other, mask(other_run)
    )
    other_1 = attend(q_other, keys_1, w_uv, "next")
    other_1, a_3, b_3 = tie(other_1, a_3, b_3)

    half = a_3.shape[0] // 2
    a_4, b_4 = step_z(a_3[half:], b_3[:half])
    keys_2 = jnp.concatenate([mine_2, theirs_2], axis=0)
    other_2 = attend(q_other, keys_2, w_uv, "next")
    other_2, a_4, b_4, w_first = tie(other_2, a_4, b_4, w_first)
    mine_3, theirs_3 = both_cores(a_3, b_3, a_4, b_4)
    keys_3 = jnp.concatenate([mine_3, theirs_3], axis=0)
    (packed,) = attend(q_other, keys_3, w_uv, "packed", before=(other_1, other_2))
    came = permute(packed, SWAP_XH)
    q_own, packed = tie(q_own, packed)
    own_2 = attend(q_own, keys_2, w_uv, "next")
    merged, own_lse = attend(q_own, keys_3, w_uv, "own", before=(own_1, own_2))

    wide = heads * VDIM
    came_lse = sum(
        came[:, wide + i * heads : wide + (i + 1) * heads].astype(F32) for i in range(3)
    )
    own_lse = own_lse[:, :heads]
    best = jnp.maximum(own_lse, came_lse)
    own_weight = jnp.exp2(own_lse - best)
    came_weight = jnp.exp2(came_lse - best)
    both = own_weight + came_weight
    spread = lambda w: jnp.repeat(w / both, VDIM, axis=1)
    values = (
        merged * spread(own_weight) + came[:, :wide].astype(F32) * spread(came_weight)
    ).astype(BF16)

    z = seq_index // 2
    y = head_index // 4
    x_lo = (head_index // 2) % 2
    odd = z % 2

    def project(*blocks):
        block = jnp.concatenate(blocks, axis=0)
        send = jnp.dot(block, w_send, preferred_element_type=F32).astype(BF16)
        came = permute(send, SWAP_CORE)
        keep = jnp.dot(block, w_keep, preferred_element_type=F32)
        return (keep + came.astype(F32)).astype(BF16)

    def across(summed, swapped):
        def take(of):
            away = (of - z // 2) % 4
            side = jnp.where((away == 1) == (swapped == 1), 2, 1)
            at = jnp.where(away == 0, 0, jnp.where(away == 2, 3, side))
            return lax.dynamic_slice_in_dim(summed, at * rows, rows, 0)

        others = (y ^ 1, (y + jnp.where(y % 2 == 1, 1, 3)) % 4, y ^ 2)
        parts = [permute(take(of), swap) for of, swap in zip(others, SWAP_Y)]
        mine = take(y).astype(F32) + sum(p.astype(F32) for p in parts)
        return mine.astype(BF16)

    w_sent, values = tie(w_out[w_half:], values)
    w_second = permute(w_sent, SWAP_XH)
    a_1, b_1 = step_z(values, values)
    a_2, b_2 = step_z(a_1, b_1)
    a_2, b_2, w_second = tie(a_2, b_2, w_second)
    a_3, b_3 = step_z(a_2, b_2)
    same = x_hi == core
    w_other = jnp.concatenate([w_first, w_second], axis=0)
    w_keep = jnp.where(same, w_out, w_other)
    w_send = jnp.where(same, w_other, w_out)
    half = rows // 2
    a_4, b_4 = step_z(a_3[half:], b_3[:half])

    odd_wave = across(project(a_1, b_1, a_3, b_3), 1 - odd)
    even_wave = across(project(values, a_2, b_2, a_4, b_4), odd)

    even = x_lo == odd
    came = permute(jnp.where(even, odd_wave, even_wave), SWAP_XL)
    mine = jnp.where(even, even_wave, odd_wave)
    return permute((mine.astype(F32) + came.astype(F32)).astype(BF16), TO_PLACE)


def solution(mesh):
    placed = (
        P("seq", None),
        P("seq", None),
        P("seq", None),
        P(),
        P("seq"),
        P(None, "head"),
        P("head", None, None),
        P("head", None, None),
        P("head", "seq"),
    )
    return jax.shard_map(
        per_device, mesh=mesh, in_specs=placed, out_specs=P("seq", "head"), check_vma=False
    )
```

profile of v0, /device:TPU:26, one launch (start us, length us, event | category | flops | bytes accessed | tf_op | source)
XLA Modules:
  0.0 138.7 jit_solution(3172057242605166517)
XLA Ops:
  4.3 2.0 %collective-permute-start = (bf16[160,640]{1,0:T(8,128)(2,1)S(1)}, bf16[160,640]{1,0:T(8,128)(2,1)S(1)}, u32[]{:S(2)}, u32[]{:S(2)}) collective-permute-start(bf16[160,640]{1,0:T(8,128)(2,1)S(1)} %get-tuple-element.42), channel_id=1, source_target_pairs={{0,32},{1,33},{2,34},{3,35},{4,36},{5,37},{6,38},{7,39},{8,40},{9,... | collective-permute-start | bytes 614408 | tf_op jit(solution)/shard_map/ppermute | solution.py:62
  6.3 4.9 %collective-permute-start.1 = (bf16[160,640]{1,0:T(8,128)(2,1)S(1)}, bf16[160,640]{1,0:T(8,128)(2,1)S(1)}, u32[]{:S(2)}, u32[]{:S(2)}) collective-permute-start(bf16[160,640]{1,0:T(8,128)(2,1)S(1)} %get-tuple-element.42), channel_id=1, source_target_pairs={{0,224},{1,225},{2,226},{3,227},{4,228},{5,229},{6,230},{7,231},{8... | collective-permute-start | bytes 614408 | tf_op jit(solution)/shard_map/ppermute | solution.py:62
  13.1 2.3 %copy-done.1 = bf16[1536,1536]{1,0:T(8,128)(2,1)S(1)} copy-done((bf16[1536,1536]{1,0:T(8,128)(2,1)S(1)}, bf16[1536,1536]{1,0:T(8,128)(2,1)}, u32[]{:S(2)}) %copy-start.1) | copy-done | bytes 4718616
  15.4 3.1 %shard_map.91.refs_0_ = bf16[8,128,640]{2,1,0:T(8,128)(2,1)S(1)} custom-call(bf16[128,1536]{1,0:T(8,128)(2,1)S(1)} %copy-done.4, bf16[1536,1536]{1,0:T(8,128)(2,1)S(1)} %copy-done.1, bf16[8,128,512]{2,1,0:T(8,128)(2,1)S(1)} %copy-done.3, f32[128,64]{1,0:T(8,128)S(1)} %get-tuple-element.103.cos_ref, f32[128,64]{1,0:T(8,128)S(1)} %get-tuple-element.104.sin_ref, ...), custom_call_target="tpu_custom_call" | custom-call | flops 92274688 | bytes 1048576 | tf_op jit(solution)/shard_map/pallas_call | solution.py:90
  21.3 4.1 %shard_map.93 = (f32[128,1024]{1,0:T(8,128)S(1)}, f32[128,128]{1,0:T(8,128)S(1)}) custom-call(bf16[8,128,640]{2,1,0:T(8,128)(2,1)S(1)} %shard_map.91.refs_0_, bf16[960,640]{1,0:T(8,128)(2,1)S(1)} %constant_dynamic-update-slice_fusion.refs_1_, bf16[8,512,128]{2,1,0:T(8,128)(2,1)S(1)} %copy-done, f32[128,128]{1,0:T(8,128)S(1)} %and_select_fusion.refs_3_), custom_call_target="tpu_custom_call" | custom-call | flops 141557760 | bytes 524288 | tf_op jit(solution)/shard_map/pallas_call | solution.py:222
  32.0 3.2 %shard_map.94.refs_0_ = bf16[8,128,640]{2,1,0:T(8,128)(2,1)S(1)} custom-call(bf16[128,1536]{1,0:T(8,128)(2,1)S(1)} %slice.47.lat_ref, bf16[1536,1536]{1,0:T(8,128)(2,1)S(1)} %copy-done.2, bf16[8,128,512]{2,1,0:T(8,128)(2,1)S(1)} %copy-done.3, f32[128,64]{1,0:T(8,128)S(1)} %pad_maximum_fusion.6.cos_ref, f32[128,64]{1,0:T(8,128)S(1)} %pad_maximum_fusion.7.sin_ref, ...), custom_call_target="tpu_custom_call" | custom-call | flops 92274688 | bytes 1048576 | tf_op jit(solution)/shard_map/pallas_call | solution.py:90
  35.1 4.1 %shard_map.95 = (f32[128,1024]{1,0:T(8,128)S(1)}, f32[128,128]{1,0:T(8,128)S(1)}) custom-call(bf16[8,128,640]{2,1,0:T(8,128)(2,1)S(1)} %shard_map.94.refs_0_, bf16[960,640]{1,0:T(8,128)(2,1)S(1)} %constant_dynamic-update-slice_fusion.refs_1_, bf16[8,512,128]{2,1,0:T(8,128)(2,1)S(1)} %copy-done), custom_call_target="tpu_custom_call" | custom-call | flops 141557760 | bytes 524288 | tf_op jit(solution)/shard_map/pallas_call | solution.py:222
  42.8 3.3 %shard_map.96 = (f32[128,1024]{1,0:T(8,128)S(1)}, f32[128,128]{1,0:T(8,128)S(1)}) custom-call(bf16[8,128,640]{2,1,0:T(8,128)(2,1)S(1)} %shard_map.94.refs_0_, bf16[640,640]{1,0:T(8,128)(2,1)S(1)} %constant_dynamic-update-slice_fusion.4.refs_1_, bf16[8,512,128]{2,1,0:T(8,128)(2,1)S(1)} %copy-done), custom_call_target="tpu_custom_call" | custom-call | flops 94371840 | bytes 524288 | tf_op jit(solution)/shard_map/pallas_call | solution.py:222
  49.3 4.6 %shard_map.97 = bf16[128,1152]{1,0:T(8,128)(2,1)S(1)} custom-call(bf16[8,128,640]{2,1,0:T(8,128)(2,1)S(1)} %shard_map.94.refs_0_, bf16[960,640]{1,0:T(8,128)(2,1)S(1)} %constant_dynamic-update-slice_fusion.7.refs_1_, bf16[8,512,128]{2,1,0:T(8,128)(2,1)S(1)} %copy-done, f32[128,1024]{1,0:T(8,128)S(1)} %get-tuple-element.62.refs_3_, ...), custom_call_target="tpu_custom_call" | custom-call | flops 141557760 | bytes 524288 | tf_op jit(solution)/shard_map/pallas_call | solution.py:222
  53.9 2.5 %collective-permute-start.13 = (bf16[128,1152]{1,0:T(8,128)(2,1)S(1)}, bf16[128,1152]{1,0:T(8,128)(2,1)S(1)}, u32[]{:S(2)}, u32[]{:S(2)}) collective-permute-start(bf16[128,1152]{1,0:T(8,128)(2,1)S(1)} %shard_map.97), channel_id=1, source_target_pairs={{0,16},{1,17},{2,18},{3,19},{4,20},{5,21},{6,22},{7,23},{8,24},{9,... | collective-permute-start | bytes 884744 | tf_op jit(solution)/shard_map/ppermute | solution.py:62
  56.4 3.3 %shard_map.98 = (f32[128,1024]{1,0:T(8,128)S(1)}, f32[128,128]{1,0:T(8,128)S(1)}) custom-call(bf16[8,128,640]{2,1,0:T(8,128)(2,1)S(1)} %shard_map.91.refs_0_, bf16[640,640]{1,0:T(8,128)(2,1)S(1)} %constant_dynamic-update-slice_fusion.4.refs_1_, bf16[8,512,128]{2,1,0:T(8,128)(2,1)S(1)} %copy-done), custom_call_target="tpu_custom_call" | custom-call | flops 94371840 | bytes 524288 | tf_op jit(solution)/shard_map/pallas_call | solution.py:222
  59.8 4.6 %shard_map.99 = (f32[128,1024]{1,0:T(8,128)S(1)}, f32[128,128]{1,0:T(8,128)S(1)}) custom-call(bf16[8,128,640]{2,1,0:T(8,128)(2,1)S(1)} %shard_map.91.refs_0_, bf16[960,640]{1,0:T(8,128)(2,1)S(1)} %constant_dynamic-update-slice_fusion.7.refs_1_, bf16[8,512,128]{2,1,0:T(8,128)(2,1)S(1)} %copy-done, f32[128,1024]{1,0:T(8,128)S(1)} %get-tuple-element.67.refs_3_, ...), custom_call_target="tpu_custom_call" | custom-call | flops 141557760 | bytes 524288 | tf_op jit(solution)/shard_map/pallas_call | solution.py:222
  67.1 2.4 %collective-permute-start.18 = (bf16[512,448]{0,1:T(8,128)(2,1)S(1)}, bf16[512,448]{0,1:T(8,128)(2,1)S(1)}, u32[]{:S(2)}, u32[]{:S(2)}) collective-permute-start(bf16[512,448]{0,1:T(8,128)(2,1)S(1)} %get-tuple-element.74), channel_id=1, source_target_pairs={{0,16},{1,17},{2,18},{3,19},{4,20},{5,21},{6,22},{7,23},{8,24},{9,... | collective-permute-start | bytes 1376264 | tf_op jit(solution)/shard_map/ppermute | solution.py:62
  69.6 5.0 %collective-permute-done.14 = bf16[128,1024]{1,0:T(8,128)(2,1)S(1)} collective-permute-done((bf16[128,1024]{1,0:T(8,128)(2,1)S(1)}, bf16[128,1024]{1,0:T(8,128)(2,1)S(1)}, u32[]{:S(2)}, u32[]{:S(2)}) %collective-permute-start.14) | collective-permute-done | bytes 262176 | tf_op jit(solution)/shard_map/ppermute | solution.py:62
  76.5 4.0 %collective-permute-done.18 = bf16[512,448]{0,1:T(8,128)(2,1)S(1)} collective-permute-done((bf16[512,448]{0,1:T(8,128)(2,1)S(1)}, bf16[512,448]{0,1:T(8,128)(2,1)S(1)}, u32[]{:S(2)}, u32[]{:S(2)}) %collective-permute-start.18) | collective-permute-done | bytes 458784 | tf_op jit(solution)/shard_map/ppermute | solution.py:62
  84.6 5.9 %collective-permute-done.19 = bf16[128,1024]{1,0:T(8,128)(2,1)S(1)} collective-permute-done((bf16[128,1024]{1,0:T(8,128)(2,1)S(1)}, bf16[128,1024]{1,0:T(8,128)(2,1)S(1)}, u32[]{:S(2)}, u32[]{:S(2)}) %collective-permute-start.19) | collective-permute-done | bytes 262176 | tf_op jit(solution)/shard_map/ppermute | solution.py:62
  95.5 2.6 %collective-permute-done.22 = bf16[64,1024]{1,0:T(8,128)(2,1)S(1)} collective-permute-done((bf16[64,1024]{1,0:T(8,128)(2,1)S(1)}, bf16[64,1024]{1,0:T(8,128)(2,1)S(1)}, u32[]{:S(2)}, u32[]{:S(2)}) %collective-permute-start.22) | collective-permute-done | bytes 131104 | tf_op jit(solution)/shard_map/ppermute | solution.py:62
  103.0 2.2 %collective-permute-start.29 = (bf16[128,448]{0,1:T(8,128)(2,1)S(1)}, bf16[128,448]{0,1:T(8,128)(2,1)S(1)}, u32[]{:S(2)}, u32[]{:S(2)}) collective-permute-start(bf16[128,448]{0,1:T(8,128)(2,1)S(1)} %get-tuple-element.86), channel_id=1, source_target_pairs={{0,12},{1,13},{2,14},{3,15},{4,8},{5,9},{6,10},{7,11},{8,4},{9,5},... | collective-permute-start | bytes 344072 | tf_op jit(solution)/shard_map/ppermute | solution.py:62
  107.1 2.5 %collective-permute-start.26 = (bf16[128,448]{0,1:T(8,128)(2,1)S(1)}, bf16[128,448]{0,1:T(8,128)(2,1)S(1)}, u32[]{:S(2)}, u32[]{:S(2)}) collective-permute-start(bf16[128,448]{0,1:T(8,128)(2,1)S(1)} %get-tuple-element.88), channel_id=1, source_target_pairs={{0,8},{1,9},{2,10},{3,11},{4,12},{5,13},{6,14},{7,15},{8,0},{9,1},... | collective-permute-start | bytes 344072 | tf_op jit(solution)/shard_map/ppermute | solution.py:62
  109.6 2.2 %collective-permute-start.25 = (bf16[128,448]{0,1:T(8,128)(2,1)S(1)}, bf16[128,448]{0,1:T(8,128)(2,1)S(1)}, u32[]{:S(2)}, u32[]{:S(2)}) collective-permute-start(bf16[128,448]{0,1:T(8,128)(2,1)S(1)} %get-tuple-element.89), channel_id=1, source_target_pairs={{0,12},{1,13},{2,14},{3,15},{4,8},{5,9},{6,10},{7,11},{8,4},{9,5},... | collective-permute-start | bytes 344072 | tf_op jit(solution)/shard_map/ppermute | solution.py:62
  113.8 2.4 %collective-permute-done.25 = bf16[128,448]{0,1:T(8,128)(2,1)S(1)} collective-permute-done((bf16[128,448]{0,1:T(8,128)(2,1)S(1)}, bf16[128,448]{0,1:T(8,128)(2,1)S(1)}, u32[]{:S(2)}, u32[]{:S(2)}) %collective-permute-start.25) | collective-permute-done | bytes 114720 | tf_op jit(solution)/shard_map/ppermute | solution.py:62
  118.7 2.9 %collective-permute-done.31 = bf16[128,448]{0,1:T(8,128)(2,1)S(1)} collective-permute-done((bf16[128,448]{0,1:T(8,128)(2,1)S(1)}, bf16[128,448]{0,1:T(8,128)(2,1)S(1)}, u32[]{:S(2)}, u32[]{:S(2)}) %collective-permute-start.31) | collective-permute-done | bytes 114720 | tf_op jit(solution)/shard_map/ppermute | solution.py:62
  121.7 5.3 %collective-permute-start.32 = (bf16[128,448]{0,1:T(8,128)(2,1)S(1)}, bf16[128,448]{0,1:T(8,128)(2,1)S(1)}, u32[]{:S(2)}, u32[]{:S(2)}) collective-permute-start(bf16[128,448]{0,1:T(8,128)(2,1)S(1)} %add_convert_fusion), channel_id=1, source_target_pairs={{0,0},{1,1},{2,32},{3,33},{4,64},{5,65},{6,96},{7,97},{8,128},{9,1... | collective-permute-start | bytes 344072 | tf_op jit(solution)/shard_map/ppermute | solution.py:62
  127.0 11.1 %collective-permute-done.32 = bf16[128,448]{0,1:T(8,128)(2,1)S(1)} collective-permute-done((bf16[128,448]{0,1:T(8,128)(2,1)S(1)}, bf16[128,448]{0,1:T(8,128)(2,1)S(1)}, u32[]{:S(2)}, u32[]{:S(2)}) %collective-permute-start.32) | collective-permute-done | bytes 114720 | tf_op jit(solution)/shard_map/ppermute | solution.py:62
  (139 shorter events, 47.2 us)
Async XLA Ops:
  4.3 14.4 %collective-permute-start = (bf16[160,640]{1,0:T(8,128)(2,1)S(1)}, bf16[160,640]{1,0:T(8,128)(2,1)S(1)}, u32[]{:S(2)}, u32[]{:S(2)}) collective-permute-start(bf16[160,640]{1,0:T(8,128)(2,1)S(1)} %get-tuple-element.42), channel_id=1, source_target_pairs={{0,32},{1,33},{2,34},{3,35},{4,36},{5,37},{6,38},{7,39},{8,40},{9,... | collective-permute-start | bytes 614408 | tf_op jit(solution)/shard_map/ppermute | solution.py:62
  6.3 12.4 %collective-permute-start.1 = (bf16[160,640]{1,0:T(8,128)(2,1)S(1)}, bf16[160,640]{1,0:T(8,128)(2,1)S(1)}, u32[]{:S(2)}, u32[]{:S(2)}) collective-permute-start(bf16[160,640]{1,0:T(8,128)(2,1)S(1)} %get-tuple-element.42), channel_id=1, source_target_pairs={{0,224},{1,225},{2,226},{3,227},{4,228},{5,229},{6,230},{7,231},{8... | collective-permute-start | bytes 614408 | tf_op jit(solution)/shard_map/ppermute | solution.py:62
  11.4 16.5 %collective-permute-start.5 = (bf16[128,1664]{1,0:T(8,128)(2,1)S(1)}, bf16[128,1664]{1,0:T(8,128)(2,1)S(1)}, u32[]{:S(2)}, u32[]{:S(2)}) collective-permute-start(bf16[128,1664]{1,0:T(8,128)(2,1)S(1)} %pad_maximum_fusion.1), channel_id=1, source_target_pairs={{0,18},{1,19},{2,16},{3,17},{4,22},{5,23},{6,20},{7,21},{8,26},{9,... | collective-permute-start | bytes 1277960 | tf_op jit(solution)/shard_map/ppermute | solution.py:62
  19.0 7.6 %collective-permute-start.3 = (bf16[160,640]{1,0:T(8,128)(2,1)S(1)}, bf16[160,640]{1,0:T(8,128)(2,1)S(1)}, u32[]{:S(2)}, u32[]{:S(2)}) collective-permute-start(bf16[160,640]{1,0:T(8,128)(2,1)S(1)} %collective-permute-done.1), channel_id=1, source_target_pairs={{0,32},{1,33},{2,34},{3,35},{4,36},{5,37},{6,38},{7,39},{8,40},{9,... | collective-permute-start | bytes 614408 | tf_op jit(solution)/shard_map/ppermute | solution.py:62
  19.1 8.8 %collective-permute-start.4 = (bf16[160,640]{1,0:T(8,128)(2,1)S(1)}, bf16[160,640]{1,0:T(8,128)(2,1)S(1)}, u32[]{:S(2)}, u32[]{:S(2)}) collective-permute-start(bf16[160,640]{1,0:T(8,128)(2,1)S(1)} %collective-permute-done), channel_id=1, source_target_pairs={{0,224},{1,225},{2,226},{3,227},{4,228},{5,229},{6,230},{7,231},{8... | collective-permute-start | bytes 614408 | tf_op jit(solution)/shard_map/ppermute | solution.py:62
  28.2 11.2 %collective-permute-start.6 = (bf16[160,640]{1,0:T(8,128)(2,1)S(1)}, bf16[160,640]{1,0:T(8,128)(2,1)S(1)}, u32[]{:S(2)}, u32[]{:S(2)}) collective-permute-start(bf16[160,640]{1,0:T(8,128)(2,1)S(1)} %collective-permute-done.4), channel_id=1, source_target_pairs={{0,32},{1,33},{2,34},{3,35},{4,36},{5,37},{6,38},{7,39},{8,40},{9,... | collective-permute-start | bytes 614408 | tf_op jit(solution)/shard_map/ppermute | solution.py:62
  28.7 10.7 %collective-permute-start.7 = (bf16[160,640]{1,0:T(8,128)(2,1)S(1)}, bf16[160,640]{1,0:T(8,128)(2,1)S(1)}, u32[]{:S(2)}, u32[]{:S(2)}) collective-permute-start(bf16[160,640]{1,0:T(8,128)(2,1)S(1)} %collective-permute-done.3), channel_id=1, source_target_pairs={{0,224},{1,225},{2,226},{3,227},{4,228},{5,229},{6,230},{7,231},{8... | collective-permute-start | bytes 614408 | tf_op jit(solution)/shard_map/ppermute | solution.py:62
  30.5 12.3 %collective-permute-start.8 = (bf16[320,640]{1,0:T(8,128)(2,1)S(1)}, bf16[320,640]{1,0:T(8,128)(2,1)S(1)}, u32[]{:S(2)}, u32[]{:S(2)}) collective-permute-start(bf16[320,640]{1,0:T(8,128)(2,1)S(1)} %pad_maximum_fusion.3), channel_id=1, source_target_pairs={{0,1},{1,0},{2,3},{3,2},{4,5},{5,4},{6,7},{7,6},{8,9},{9,8},{10,11... | collective-permute-start | bytes 1228808 | tf_op jit(solution)/shard_map/ppermute | solution.py:62
  30.7 16.3 %collective-permute-start.11 = (bf16[512,448]{0,1:T(8,128)(2,1)S(1)}, bf16[512,448]{0,1:T(8,128)(2,1)S(1)}, u32[]{:S(2)}, u32[]{:S(2)}) collective-permute-start(bf16[512,448]{0,1:T(8,128)(2,1)S(1)} %get-tuple-element.59), channel_id=1, source_target_pairs={{0,16},{1,17},{2,18},{3,19},{4,20},{5,21},{6,22},{7,23},{8,24},{9,... | collective-permute-start | bytes 1376264 | tf_op jit(solution)/shard_map/ppermute | solution.py:62
  39.4 6.7 %collective-permute-start.9 = (bf16[80,640]{1,0:T(8,128)(2,1)S(1)}, bf16[80,640]{1,0:T(8,128)(2,1)S(1)}, u32[]{:S(2)}, u32[]{:S(2)}) collective-permute-start(bf16[80,640]{1,0:T(8,128)(2,1)S(1)} %slice.51), channel_id=1, source_target_pairs={{0,32},{1,33},{2,34},{3,35},{4,36},{5,37},{6,38},{7,39},{8,40},{9,... | collective-permute-start | bytes 307208 | tf_op jit(solution)/shard_map/ppermute | solution.py:62
  53.9 10.7 %collective-permute-start.13 = (bf16[128,1152]{1,0:T(8,128)(2,1)S(1)}, bf16[128,1152]{1,0:T(8,128)(2,1)S(1)}, u32[]{:S(2)}, u32[]{:S(2)}) collective-permute-start(bf16[128,1152]{1,0:T(8,128)(2,1)S(1)} %shard_map.97), channel_id=1, source_target_pairs={{0,16},{1,17},{2,18},{3,19},{4,20},{5,21},{6,22},{7,23},{8,24},{9,... | collective-permute-start | bytes 884744 | tf_op jit(solution)/shard_map/ppermute | solution.py:62
  65.4 9.2 %collective-permute-start.14 = (bf16[128,1024]{1,0:T(8,128)(2,1)S(1)}, bf16[128,1024]{1,0:T(8,128)(2,1)S(1)}, u32[]{:S(2)}, u32[]{:S(2)}) collective-permute-start(bf16[128,1024]{1,0:T(8,128)(2,1)S(1)} %fusion.3), channel_id=1, source_target_pairs={{0,224},{1,225},{2,226},{3,227},{4,228},{5,229},{6,230},{7,231},{8... | collective-permute-start | bytes 786440 | tf_op jit(solution)/shard_map/ppermute | solution.py:62
  67.1 7.6 %collective-permute-start.16 = (bf16[128,1024]{1,0:T(8,128)(2,1)S(1)}, bf16[128,1024]{1,0:T(8,128)(2,1)S(1)}, u32[]{:S(2)}, u32[]{:S(2)}) collective-permute-start(bf16[128,1024]{1,0:T(8,128)(2,1)S(1)} %fusion.3), channel_id=1, source_target_pairs={{0,32},{1,33},{2,34},{3,35},{4,36},{5,37},{6,38},{7,39},{8,40},{9,... | collective-permute-start | bytes 786440 | tf_op jit(solution)/shard_map/ppermute | solution.py:62
  67.1 13.3 %collective-permute-start.18 = (bf16[512,448]{0,1:T(8,128)(2,1)S(1)}, bf16[512,448]{0,1:T(8,128)(2,1)S(1)}, u32[]{:S(2)}, u32[]{:S(2)}) collective-permute-start(bf16[512,448]{0,1:T(8,128)(2,1)S(1)} %get-tuple-element.74), channel_id=1, source_target_pairs={{0,16},{1,17},{2,18},{3,19},{4,20},{5,21},{6,22},{7,23},{8,24},{9,... | collective-permute-start | bytes 1376264 | tf_op jit(solution)/shard_map/ppermute | solution.py:62
  74.6 7.0 %collective-permute-start.15 = (bf16[128,1024]{1,0:T(8,128)(2,1)S(1)}, bf16[128,1024]{1,0:T(8,128)(2,1)S(1)}, u32[]{:S(2)}, u32[]{:S(2)}) collective-permute-start(bf16[128,1024]{1,0:T(8,128)(2,1)S(1)} %collective-permute-done.14), channel_id=1, source_target_pairs={{0,32},{1,33},{2,34},{3,35},{4,36},{5,37},{6,38},{7,39},{8,40},{9,... | collective-permute-start | bytes 786440 | tf_op jit(solution)/shard_map/ppermute | solution.py:62
  74.8 8.1 %collective-permute-start.17 = (bf16[128,1024]{1,0:T(8,128)(2,1)S(1)}, bf16[128,1024]{1,0:T(8,128)(2,1)S(1)}, u32[]{:S(2)}, u32[]{:S(2)}) collective-permute-start(bf16[128,1024]{1,0:T(8,128)(2,1)S(1)} %collective-permute-done.16), channel_id=1, source_target_pairs={{0,224},{1,225},{2,226},{3,227},{4,228},{5,229},{6,230},{7,231},{8... | collective-permute-start | bytes 786440 | tf_op jit(solution)/shard_map/ppermute | solution.py:62
  82.9 7.6 %collective-permute-start.19 = (bf16[128,1024]{1,0:T(8,128)(2,1)S(1)}, bf16[128,1024]{1,0:T(8,128)(2,1)S(1)}, u32[]{:S(2)}, u32[]{:S(2)}) collective-permute-start(bf16[128,1024]{1,0:T(8,128)(2,1)S(1)} %collective-permute-done.15), channel_id=1, source_target_pairs={{0,224},{1,225},{2,226},{3,227},{4,228},{5,229},{6,230},{7,231},{8... | collective-permute-start | bytes 786440 | tf_op jit(solution)/shard_map/ppermute | solution.py:62
  84.5 7.4 %collective-permute-start.21 = (bf16[128,1024]{1,0:T(8,128)(2,1)S(1)}, bf16[128,1024]{1,0:T(8,128)(2,1)S(1)}, u32[]{:S(2)}, u32[]{:S(2)}) collective-permute-start(bf16[128,1024]{1,0:T(8,128)(2,1)S(1)} %collective-permute-done.17), channel_id=1, source_target_pairs={{0,32},{1,33},{2,34},{3,35},{4,36},{5,37},{6,38},{7,39},{8,40},{9,... | collective-permute-start | bytes 786440 | tf_op jit(solution)/shard_map/ppermute | solution.py:62
  101.7 10.1 %collective-permute-start.30 = (bf16[128,448]{0,1:T(8,128)(2,1)S(1)}, bf16[128,448]{0,1:T(8,128)(2,1)S(1)}, u32[]{:S(2)}, u32[]{:S(2)}) collective-permute-start(bf16[128,448]{0,1:T(8,128)(2,1)S(1)} %get-tuple-element.85), channel_id=1, source_target_pairs={{0,8},{1,9},{2,10},{3,11},{4,12},{5,13},{6,14},{7,15},{8,0},{9,1},... | collective-permute-start | bytes 344072 | tf_op jit(solution)/shard_map/ppermute | solution.py:62
  103.0 8.8 %collective-permute-start.29 = (bf16[128,448]{0,1:T(8,128)(2,1)S(1)}, bf16[128,448]{0,1:T(8,128)(2,1)S(1)}, u32[]{:S(2)}, u32[]{:S(2)}) collective-permute-start(bf16[128,448]{0,1:T(8,128)(2,1)S(1)} %get-tuple-element.86), channel_id=1, source_target_pairs={{0,12},{1,13},{2,14},{3,15},{4,8},{5,9},{6,10},{7,11},{8,4},{9,5},... | collective-permute-start | bytes 344072 | tf_op jit(solution)/shard_map/ppermute | solution.py:62
  105.2 6.6 %collective-permute-start.28 = (bf16[128,448]{0,1:T(8,128)(2,1)S(1)}, bf16[128,448]{0,1:T(8,128)(2,1)S(1)}, u32[]{:S(2)}, u32[]{:S(2)}) collective-permute-start(bf16[128,448]{0,1:T(8,128)(2,1)S(1)} %get-tuple-element.84), channel_id=1, source_target_pairs={{0,4},{1,5},{2,6},{3,7},{4,0},{5,1},{6,2},{7,3},{8,12},{9,13},{10,... | collective-permute-start | bytes 344072 | tf_op jit(solution)/shard_map/ppermute | solution.py:62
  107.1 6.7 %collective-permute-start.26 = (bf16[128,448]{0,1:T(8,128)(2,1)S(1)}, bf16[128,448]{0,1:T(8,128)(2,1)S(1)}, u32[]{:S(2)}, u32[]{:S(2)}) collective-permute-start(bf16[128,448]{0,1:T(8,128)(2,1)S(1)} %get-tuple-element.88), channel_id=1, source_target_pairs={{0,8},{1,9},{2,10},{3,11},{4,12},{5,13},{6,14},{7,15},{8,0},{9,1},... | collective-permute-start | bytes 344072 | tf_op jit(solution)/shard_map/ppermute | solution.py:62
  109.6 6.5 %collective-permute-start.25 = (bf16[128,448]{0,1:T(8,128)(2,1)S(1)}, bf16[128,448]{0,1:T(8,128)(2,1)S(1)}, u32[]{:S(2)}, u32[]{:S(2)}) collective-permute-start(bf16[128,448]{0,1:T(8,128)(2,1)S(1)} %get-tuple-element.89), channel_id=1, source_target_pairs={{0,12},{1,13},{2,14},{3,15},{4,8},{5,9},{6,10},{7,11},{8,4},{9,5},... | collective-permute-start | bytes 344072 | tf_op jit(solution)/shard_map/ppermute | solution.py:62
  121.7 16.4 %collective-permute-start.32 = (bf16[128,448]{0,1:T(8,128)(2,1)S(1)}, bf16[128,448]{0,1:T(8,128)(2,1)S(1)}, u32[]{:S(2)}, u32[]{:S(2)}) collective-permute-start(bf16[128,448]{0,1:T(8,128)(2,1)S(1)} %add_convert_fusion), channel_id=1, source_target_pairs={{0,0},{1,1},{2,32},{3,33},{4,64},{5,65},{6,96},{7,97},{8,128},{9,1... | collective-permute-start | bytes 344072 | tf_op jit(solution)/shard_map/ppermute | solution.py:62
  (21 other events, 95.7 us)
where the time goes:
time: 139 us
  waiting for transfers between devices  46.5 us (33%)
  starting transfers between devices  44.5 us (32%)
  Pallas kernels  30.7 us (22%)
  local copies, waits for them, and re-layouts  7.64 us (5%)
  matrix products  5.76 us (4%)
  other arithmetic  2.92 us (2%)
    ppermute x33, waiting for transfers between devices, permute(): return lax.ppermute(x, AXES, perm)  46.5 us
    ppermute x33, starting transfers between devices, permute(): return lax.ppermute(x, AXES, perm)  44.5 us
    pallas_call x6, Pallas kernels, attend(): pl.pallas_call(functools.partial(attend_kernel, stack, kind), in_specs=[s...  24.2 us
    unnamed x43, local copies, waits for them, and re-layouts  6.47 us
    pallas_call x2, Pallas kernels, queries(): pl.pallas_call(query_kernel, grid=(heads // 2,), in_specs=[pl.BlockSpec(l...  6.29 us
    dot_general x2, matrix products, project(): keep = jnp.dot(block, w_keep, preferred_element_type=F32)  3.51 us
  transfers between devices with their start and end apart: 33, of which 19 were waited for; matrix products, arithmetic and copies ran while one was open for 5% of the time, Pallas kernels for 19%

commit v1 on v0

--- a/solution.py
+++ b/solution.py
@@ -191,9 +191,11 @@
         return finish(group, (accum / total).astype(BF16), top + jnp.log2(total), kept)
 
     top_ref[...] = functools.reduce(jnp.maximum, [score(0, 0, cut) for cut in cuts])
-    kept = lax.fori_loop(
-        0, groups - 1, lambda g, kept: turn(g, kept, True), jnp.zeros((rows, 128), F32)
-    )
+    kept = jnp.zeros((rows, 128), F32)
+    if groups == 2:
+        kept = turn(0, kept, True)
+    else:
+        kept = lax.fori_loop(0, groups - 1, lambda g, kept: turn(g, kept, True), kept)
     kept = turn(groups - 1, kept, False)
     if kind != "packed":
         refs[1][...] = kept
@@ -208,7 +210,7 @@
 def attend(q, keys, w_uv, kind, bias=None, before=()):
     heads, rows, _ = q.shape
     count = keys.shape[0]
-    stack = 2
+    stack = 4 if kind == "packed" else 2
     operands = [q, keys, w_uv]
     if bias is not None:
         operands.append(bias)

time: 139 us -> 138 us (level)
  no operation moved by 1% of the time
where the time goes in v1:
time: 138 us
  waiting for transfers between devices  46.8 us (34%)
  starting transfers between devices  44.3 us (32%)
  Pallas kernels  29.8 us (22%)
  local copies, waits for them, and re-layouts  7.64 us (6%)
  matrix products  5.75 us (4%)
  other arithmetic  2.92 us (2%)
    ppermute x33, waiting for transfers between devices, permute(): return lax.ppermute(x, AXES, perm)  46.8 us
    ppermute x33, starting transfers between devices, permute(): return lax.ppermute(x, AXES, perm)  44.3 us
    pallas_call x6, Pallas kernels, attend(): pl.pallas_call(functools.partial(attend_kernel, stack, kind), in_specs=[s...  23.2 us
    unnamed x43, local copies, waits for them, and re-layouts  6.47 us
    pallas_call x2, Pallas kernels, queries(): pl.pallas_call(query_kernel, grid=(heads // 2,), in_specs=[pl.BlockSpec(l...  6.29 us
    dot_general x2, matrix products, project(): keep = jnp.dot(block, w_keep, preferred_element_type=F32)  3.51 us
  transfers between devices with their start and end apart: 33, of which 19 were waited for; matrix products, arithmetic and copies ran while one was open for 5% of the time, Pallas kernels for 19%

profile of v1, /device:TPU:26, one launch (start us, length us, event | category | flops | bytes accessed | tf_op | source)
XLA Modules:
  0.0 137.7 jit_solution(3862562196544879711)
XLA Ops:
  4.3 2.0 %collective-permute-start = (bf16[160,640]{1,0:T(8,128)(2,1)S(1)}, bf16[160,640]{1,0:T(8,128)(2,1)S(1)}, u32[]{:S(2)}, u32[]{:S(2)}) collective-permute-start(bf16[160,640]{1,0:T(8,128)(2,1)S(1)} %get-tuple-element.42), channel_id=1, source_target_pairs={{0,32},{1,33},{2,34},{3,35},{4,36},{5,37},{6,38},{7,39},{8,40},{9,... | collective-permute-start | bytes 614408 | tf_op jit(solution)/shard_map/ppermute | solution.py:62
  6.3 4.9 %collective-permute-start.1 = (bf16[160,640]{1,0:T(8,128)(2,1)S(1)}, bf16[160,640]{1,0:T(8,128)(2,1)S(1)}, u32[]{:S(2)}, u32[]{:S(2)}) collective-permute-start(bf16[160,640]{1,0:T(8,128)(2,1)S(1)} %get-tuple-element.42), channel_id=1, source_target_pairs={{0,224},{1,225},{2,226},{3,227},{4,228},{5,229},{6,230},{7,231},{8... | collective-permute-start | bytes 614408 | tf_op jit(solution)/shard_map/ppermute | solution.py:62
  13.1 2.3 %copy-done.1 = bf16[1536,1536]{1,0:T(8,128)(2,1)S(1)} copy-done((bf16[1536,1536]{1,0:T(8,128)(2,1)S(1)}, bf16[1536,1536]{1,0:T(8,128)(2,1)}, u32[]{:S(2)}) %copy-start.1) | copy-done | bytes 4718616
  15.4 3.1 %shard_map.91.refs_0_ = bf16[8,128,640]{2,1,0:T(8,128)(2,1)S(1)} custom-call(bf16[128,1536]{1,0:T(8,128)(2,1)S(1)} %copy-done.4, bf16[1536,1536]{1,0:T(8,128)(2,1)S(1)} %copy-done.1, bf16[8,128,512]{2,1,0:T(8,128)(2,1)S(1)} %copy-done.3, f32[128,64]{1,0:T(8,128)S(1)} %get-tuple-element.103.cos_ref, f32[128,64]{1,0:T(8,128)S(1)} %get-tuple-element.104.sin_ref, ...), custom_call_target="tpu_custom_call" | custom-call | flops 92274688 | bytes 1048576 | tf_op jit(solution)/shard_map/pallas_call | solution.py:90
  21.3 4.1 %shard_map.93 = (f32[128,1024]{1,0:T(8,128)S(1)}, f32[128,128]{1,0:T(8,128)S(1)}) custom-call(bf16[8,128,640]{2,1,0:T(8,128)(2,1)S(1)} %shard_map.91.refs_0_, bf16[960,640]{1,0:T(8,128)(2,1)S(1)} %constant_dynamic-update-slice_fusion.refs_1_, bf16[8,512,128]{2,1,0:T(8,128)(2,1)S(1)} %copy-done, f32[128,128]{1,0:T(8,128)S(1)} %and_select_fusion.refs_3_), custom_call_target="tpu_custom_call" | custom-call | flops 141557760 | bytes 524288 | tf_op jit(solution)/shard_map/pallas_call | solution.py:224
  32.0 3.2 %shard_map.94.refs_0_ = bf16[8,128,640]{2,1,0:T(8,128)(2,1)S(1)} custom-call(bf16[128,1536]{1,0:T(8,128)(2,1)S(1)} %slice.47.lat_ref, bf16[1536,1536]{1,0:T(8,128)(2,1)S(1)} %copy-done.2, bf16[8,128,512]{2,1,0:T(8,128)(2,1)S(1)} %copy-done.3, f32[128,64]{1,0:T(8,128)S(1)} %pad_maximum_fusion.6.cos_ref, f32[128,64]{1,0:T(8,128)S(1)} %pad_maximum_fusion.7.sin_ref, ...), custom_call_target="tpu_custom_call" | custom-call | flops 92274688 | bytes 1048576 | tf_op jit(solution)/shard_map/pallas_call | solution.py:90
  35.1 4.1 %shard_map.95 = (f32[128,1024]{1,0:T(8,128)S(1)}, f32[128,128]{1,0:T(8,128)S(1)}) custom-call(bf16[8,128,640]{2,1,0:T(8,128)(2,1)S(1)} %shard_map.94.refs_0_, bf16[960,640]{1,0:T(8,128)(2,1)S(1)} %constant_dynamic-update-slice_fusion.refs_1_, bf16[8,512,128]{2,1,0:T(8,128)(2,1)S(1)} %copy-done), custom_call_target="tpu_custom_call" | custom-call | flops 141557760 | bytes 524288 | tf_op jit(solution)/shard_map/pallas_call | solution.py:224
  42.8 3.3 %shard_map.96 = (f32[128,1024]{1,0:T(8,128)S(1)}, f32[128,128]{1,0:T(8,128)S(1)}) custom-call(bf16[8,128,640]{2,1,0:T(8,128)(2,1)S(1)} %shard_map.94.refs_0_, bf16[640,640]{1,0:T(8,128)(2,1)S(1)} %constant_dynamic-update-slice_fusion.4.refs_1_, bf16[8,512,128]{2,1,0:T(8,128)(2,1)S(1)} %copy-done), custom_call_target="tpu_custom_call" | custom-call | flops 94371840 | bytes 524288 | tf_op jit(solution)/shard_map/pallas_call | solution.py:224
  49.3 3.7 %shard_map.97 = bf16[128,1152]{1,0:T(8,128)(2,1)S(1)} custom-call(bf16[8,128,640]{2,1,0:T(8,128)(2,1)S(1)} %shard_map.94.refs_0_, bf16[960,640]{1,0:T(8,128)(2,1)S(1)} %constant_dynamic-update-slice_fusion.7.refs_1_, bf16[8,512,128]{2,1,0:T(8,128)(2,1)S(1)} %copy-done, f32[128,1024]{1,0:T(8,128)S(1)} %get-tuple-element.62.refs_3_, ...), custom_call_target="tpu_custom_call" | custom-call | flops 141557760 | bytes 524288 | tf_op jit(solution)/shard_map/pallas_call | solution.py:224
  53.0 2.5 %collective-permute-start.13 = (bf16[128,1152]{1,0:T(8,128)(2,1)S(1)}, bf16[128,1152]{1,0:T(8,128)(2,1)S(1)}, u32[]{:S(2)}, u32[]{:S(2)}) collective-permute-start(bf16[128,1152]{1,0:T(8,128)(2,1)S(1)} %shard_map.97), channel_id=1, source_target_pairs={{0,16},{1,17},{2,18},{3,19},{4,20},{5,21},{6,22},{7,23},{8,24},{9,... | collective-permute-start | bytes 884744 | tf_op jit(solution)/shard_map/ppermute | solution.py:62
  55.5 3.3 %shard_map.98 = (f32[128,1024]{1,0:T(8,128)S(1)}, f32[128,128]{1,0:T(8,128)S(1)}) custom-call(bf16[8,128,640]{2,1,0:T(8,128)(2,1)S(1)} %shard_map.91.refs_0_, bf16[640,640]{1,0:T(8,128)(2,1)S(1)} %constant_dynamic-update-slice_fusion.4.refs_1_, bf16[8,512,128]{2,1,0:T(8,128)(2,1)S(1)} %copy-done), custom_call_target="tpu_custom_call" | custom-call | flops 94371840 | bytes 524288 | tf_op jit(solution)/shard_map/pallas_call | solution.py:224
  58.8 4.6 %shard_map.99 = (f32[128,1024]{1,0:T(8,128)S(1)}, f32[128,128]{1,0:T(8,128)S(1)}) custom-call(bf16[8,128,640]{2,1,0:T(8,128)(2,1)S(1)} %shard_map.91.refs_0_, bf16[960,640]{1,0:T(8,128)(2,1)S(1)} %constant_dynamic-update-slice_fusion.7.refs_1_, bf16[8,512,128]{2,1,0:T(8,128)(2,1)S(1)} %copy-done, f32[128,1024]{1,0:T(8,128)S(1)} %get-tuple-element.67.refs_3_, ...), custom_call_target="tpu_custom_call" | custom-call | flops 141557760 | bytes 524288 | tf_op jit(solution)/shard_map/pallas_call | solution.py:224
  66.2 2.4 %collective-permute-start.18 = (bf16[512,448]{0,1:T(8,128)(2,1)S(1)}, bf16[512,448]{0,1:T(8,128)(2,1)S(1)}, u32[]{:S(2)}, u32[]{:S(2)}) collective-permute-start(bf16[512,448]{0,1:T(8,128)(2,1)S(1)} %get-tuple-element.74), channel_id=1, source_target_pairs={{0,16},{1,17},{2,18},{3,19},{4,20},{5,21},{6,22},{7,23},{8,24},{9,... | collective-permute-start | bytes 1376264 | tf_op jit(solution)/shard_map/ppermute | solution.py:62
  68.6 5.0 %collective-permute-done.14 = bf16[128,1024]{1,0:T(8,128)(2,1)S(1)} collective-permute-done((bf16[128,1024]{1,0:T(8,128)(2,1)S(1)}, bf16[128,1024]{1,0:T(8,128)(2,1)S(1)}, u32[]{:S(2)}, u32[]{:S(2)}) %collective-permute-start.14) | collective-permute-done | bytes 262176 | tf_op jit(solution)/shard_map/ppermute | solution.py:62
  75.5 4.1 %collective-permute-done.18 = bf16[512,448]{0,1:T(8,128)(2,1)S(1)} collective-permute-done((bf16[512,448]{0,1:T(8,128)(2,1)S(1)}, bf16[512,448]{0,1:T(8,128)(2,1)S(1)}, u32[]{:S(2)}, u32[]{:S(2)}) %collective-permute-start.18) | collective-permute-done | bytes 458784 | tf_op jit(solution)/shard_map/ppermute | solution.py:62
  83.6 5.8 %collective-permute-done.19 = bf16[128,1024]{1,0:T(8,128)(2,1)S(1)} collective-permute-done((bf16[128,1024]{1,0:T(8,128)(2,1)S(1)}, bf16[128,1024]{1,0:T(8,128)(2,1)S(1)}, u32[]{:S(2)}, u32[]{:S(2)}) %collective-permute-start.19) | collective-permute-done | bytes 262176 | tf_op jit(solution)/shard_map/ppermute | solution.py:62
  94.5 2.7 %collective-permute-done.22 = bf16[64,1024]{1,0:T(8,128)(2,1)S(1)} collective-permute-done((bf16[64,1024]{1,0:T(8,128)(2,1)S(1)}, bf16[64,1024]{1,0:T(8,128)(2,1)S(1)}, u32[]{:S(2)}, u32[]{:S(2)}) %collective-permute-start.22) | collective-permute-done | bytes 131104 | tf_op jit(solution)/shard_map/ppermute | solution.py:62
  102.1 2.2 %collective-permute-start.29 = (bf16[128,448]{0,1:T(8,128)(2,1)S(1)}, bf16[128,448]{0,1:T(8,128)(2,1)S(1)}, u32[]{:S(2)}, u32[]{:S(2)}) collective-permute-start(bf16[128,448]{0,1:T(8,128)(2,1)S(1)} %get-tuple-element.86), channel_id=1, source_target_pairs={{0,12},{1,13},{2,14},{3,15},{4,8},{5,9},{6,10},{7,11},{8,4},{9,5},... | collective-permute-start | bytes 344072 | tf_op jit(solution)/shard_map/ppermute | solution.py:62
  106.1 2.6 %collective-permute-start.26 = (bf16[128,448]{0,1:T(8,128)(2,1)S(1)}, bf16[128,448]{0,1:T(8,128)(2,1)S(1)}, u32[]{:S(2)}, u32[]{:S(2)}) collective-permute-start(bf16[128,448]{0,1:T(8,128)(2,1)S(1)} %get-tuple-element.88), channel_id=1, source_target_pairs={{0,8},{1,9},{2,10},{3,11},{4,12},{5,13},{6,14},{7,15},{8,0},{9,1},... | collective-permute-start | bytes 344072 | tf_op jit(solution)/shard_map/ppermute | solution.py:62
  108.7 2.2 %collective-permute-start.25 = (bf16[128,448]{0,1:T(8,128)(2,1)S(1)}, bf16[128,448]{0,1:T(8,128)(2,1)S(1)}, u32[]{:S(2)}, u32[]{:S(2)}) collective-permute-start(bf16[128,448]{0,1:T(8,128)(2,1)S(1)} %get-tuple-element.89), channel_id=1, source_target_pairs={{0,12},{1,13},{2,14},{3,15},{4,8},{5,9},{6,10},{7,11},{8,4},{9,5},... | collective-permute-start | bytes 344072 | tf_op jit(solution)/shard_map/ppermute | solution.py:62
  112.9 2.4 %collective-permute-done.25 = bf16[128,448]{0,1:T(8,128)(2,1)S(1)} collective-permute-done((bf16[128,448]{0,1:T(8,128)(2,1)S(1)}, bf16[128,448]{0,1:T(8,128)(2,1)S(1)}, u32[]{:S(2)}, u32[]{:S(2)}) %collective-permute-start.25) | collective-permute-done | bytes 114720 | tf_op jit(solution)/shard_map/ppermute | solution.py:62
  117.7 3.0 %collective-permute-done.31 = bf16[128,448]{0,1:T(8,128)(2,1)S(1)} collective-permute-done((bf16[128,448]{0,1:T(8,128)(2,1)S(1)}, bf16[128,448]{0,1:T(8,128)(2,1)S(1)}, u32[]{:S(2)}, u32[]{:S(2)}) %collective-permute-start.31) | collective-permute-done | bytes 114720 | tf_op jit(solution)/shard_map/ppermute | solution.py:62
  120.7 5.3 %collective-permute-start.32 = (bf16[128,448]{0,1:T(8,128)(2,1)S(1)}, bf16[128,448]{0,1:T(8,128)(2,1)S(1)}, u32[]{:S(2)}, u32[]{:S(2)}) collective-permute-start(bf16[128,448]{0,1:T(8,128)(2,1)S(1)} %add_convert_fusion), channel_id=1, source_target_pairs={{0,0},{1,1},{2,32},{3,33},{4,64},{5,65},{6,96},{7,97},{8,128},{9,1... | collective-permute-start | bytes 344072 | tf_op jit(solution)/shard_map/ppermute | solution.py:62
  126.0 11.1 %collective-permute-done.32 = bf16[128,448]{0,1:T(8,128)(2,1)S(1)} collective-permute-done((bf16[128,448]{0,1:T(8,128)(2,1)S(1)}, bf16[128,448]{0,1:T(8,128)(2,1)S(1)}, u32[]{:S(2)}, u32[]{:S(2)}) %collective-permute-start.32) | collective-permute-done | bytes 114720 | tf_op jit(solution)/shard_map/ppermute | solution.py:62
  (139 shorter events, 47.2 us)
Async XLA Ops:
  4.3 14.4 %collective-permute-start = (bf16[160,640]{1,0:T(8,128)(2,1)S(1)}, bf16[160,640]{1,0:T(8,128)(2,1)S(1)}, u32[]{:S(2)}, u32[]{:S(2)}) collective-permute-start(bf16[160,640]{1,0:T(8,128)(2,1)S(1)} %get-tuple-element.42), channel_id=1, source_target_pairs={{0,32},{1,33},{2,34},{3,35},{4,36},{5,37},{6,38},{7,39},{8,40},{9,... | collective-permute-start | bytes 614408 | tf_op jit(solution)/shard_map/ppermute | solution.py:62
  6.3 12.4 %collective-permute-start.1 = (bf16[160,640]{1,0:T(8,128)(2,1)S(1)}, bf16[160,640]{1,0:T(8,128)(2,1)S(1)}, u32[]{:S(2)}, u32[]{:S(2)}) collective-permute-start(bf16[160,640]{1,0:T(8,128)(2,1)S(1)} %get-tuple-element.42), channel_id=1, source_target_pairs={{0,224},{1,225},{2,226},{3,227},{4,228},{5,229},{6,230},{7,231},{8... | collective-permute-start | bytes 614408 | tf_op jit(solution)/shard_map/ppermute | solution.py:62
  11.4 16.5 %collective-permute-start.5 = (bf16[128,1664]{1,0:T(8,128)(2,1)S(1)}, bf16[128,1664]{1,0:T(8,128)(2,1)S(1)}, u32[]{:S(2)}, u32[]{:S(2)}) collective-permute-start(bf16[128,1664]{1,0:T(8,128)(2,1)S(1)} %pad_maximum_fusion.1), channel_id=1, source_target_pairs={{0,18},{1,19},{2,16},{3,17},{4,22},{5,23},{6,20},{7,21},{8,26},{9,... | collective-permute-start | bytes 1277960 | tf_op jit(solution)/shard_map/ppermute | solution.py:62
  19.0 7.6 %collective-permute-start.3 = (bf16[160,640]{1,0:T(8,128)(2,1)S(1)}, bf16[160,640]{1,0:T(8,128)(2,1)S(1)}, u32[]{:S(2)}, u32[]{:S(2)}) collective-permute-start(bf16[160,640]{1,0:T(8,128)(2,1)S(1)} %collective-permute-done.1), channel_id=1, source_target_pairs={{0,32},{1,33},{2,34},{3,35},{4,36},{5,37},{6,38},{7,39},{8,40},{9,... | collective-permute-start | bytes 614408 | tf_op jit(solution)/shard_map/ppermute | solution.py:62
  19.1 8.8 %collective-permute-start.4 = (bf16[160,640]{1,0:T(8,128)(2,1)S(1)}, bf16[160,640]{1,0:T(8,128)(2,1)S(1)}, u32[]{:S(2)}, u32[]{:S(2)}) collective-permute-start(bf16[160,640]{1,0:T(8,128)(2,1)S(1)} %collective-permute-done), channel_id=1, source_target_pairs={{0,224},{1,225},{2,226},{3,227},{4,228},{5,229},{6,230},{7,231},{8... | collective-permute-start | bytes 614408 | tf_op jit(solution)/shard_map/ppermute | solution.py:62
  28.2 11.2 %collective-permute-start.6 = (bf16[160,640]{1,0:T(8,128)(2,1)S(1)}, bf16[160,640]{1,0:T(8,128)(2,1)S(1)}, u32[]{:S(2)}, u32[]{:S(2)}) collective-permute-start(bf16[160,640]{1,0:T(8,128)(2,1)S(1)} %collective-permute-done.4), channel_id=1, source_target_pairs={{0,32},{1,33},{2,34},{3,35},{4,36},{5,37},{6,38},{7,39},{8,40},{9,... | collective-permute-start | bytes 614408 | tf_op jit(solution)/shard_map/ppermute | solution.py:62
  28.7 10.7 %collective-permute-start.7 = (bf16[160,640]{1,0:T(8,128)(2,1)S(1)}, bf16[160,640]{1,0:T(8,128)(2,1)S(1)}, u32[]{:S(2)}, u32[]{:S(2)}) collective-permute-start(bf16[160,640]{1,0:T(8,128)(2,1)S(1)} %collective-permute-done.3), channel_id=1, source_target_pairs={{0,224},{1,225},{2,226},{3,227},{4,228},{5,229},{6,230},{7,231},{8... | collective-permute-start | bytes 614408 | tf_op jit(solution)/shard_map/ppermute | solution.py:62
  30.5 12.3 %collective-permute-start.8 = (bf16[320,640]{1,0:T(8,128)(2,1)S(1)}, bf16[320,640]{1,0:T(8,128)(2,1)S(1)}, u32[]{:S(2)}, u32[]{:S(2)}) collective-permute-start(bf16[320,640]{1,0:T(8,128)(2,1)S(1)} %pad_maximum_fusion.3), channel_id=1, source_target_pairs={{0,1},{1,0},{2,3},{3,2},{4,5},{5,4},{6,7},{7,6},{8,9},{9,8},{10,11... | collective-permute-start | bytes 1228808 | tf_op jit(solution)/shard_map/ppermute | solution.py:62
  30.7 16.3 %collective-permute-start.11 = (bf16[512,448]{0,1:T(8,128)(2,1)S(1)}, bf16[512,448]{0,1:T(8,128)(2,1)S(1)}, u32[]{:S(2)}, u32[]{:S(2)}) collective-permute-start(bf16[512,448]{0,1:T(8,128)(2,1)S(1)} %get-tuple-element.59), channel_id=1, source_target_pairs={{0,16},{1,17},{2,18},{3,19},{4,20},{5,21},{6,22},{7,23},{8,24},{9,... | collective-permute-start | bytes 1376264 | tf_op jit(solution)/shard_map/ppermute | solution.py:62
  39.4 6.7 %collective-permute-start.9 = (bf16[80,640]{1,0:T(8,128)(2,1)S(1)}, bf16[80,640]{1,0:T(8,128)(2,1)S(1)}, u32[]{:S(2)}, u32[]{:S(2)}) collective-permute-start(bf16[80,640]{1,0:T(8,128)(2,1)S(1)} %slice.51), channel_id=1, source_target_pairs={{0,32},{1,33},{2,34},{3,35},{4,36},{5,37},{6,38},{7,39},{8,40},{9,... | collective-permute-start | bytes 307208 | tf_op jit(solution)/shard_map/ppermute | solution.py:62
  53.0 10.6 %collective-permute-start.13 = (bf16[128,1152]{1,0:T(8,128)(2,1)S(1)}, bf16[128,1152]{1,0:T(8,128)(2,1)S(1)}, u32[]{:S(2)}, u32[]{:S(2)}) collective-permute-start(bf16[128,1152]{1,0:T(8,128)(2,1)S(1)} %shard_map.97), channel_id=1, source_target_pairs={{0,16},{1,17},{2,18},{3,19},{4,20},{5,21},{6,22},{7,23},{8,24},{9,... | collective-permute-start | bytes 884744 | tf_op jit(solution)/shard_map/ppermute | solution.py:62
  64.4 9.2 %collective-permute-start.14 = (bf16[128,1024]{1,0:T(8,128)(2,1)S(1)}, bf16[128,1024]{1,0:T(8,128)(2,1)S(1)}, u32[]{:S(2)}, u32[]{:S(2)}) collective-permute-start(bf16[128,1024]{1,0:T(8,128)(2,1)S(1)} %fusion.3), channel_id=1, source_target_pairs={{0,224},{1,225},{2,226},{3,227},{4,228},{5,229},{6,230},{7,231},{8... | collective-permute-start | bytes 786440 | tf_op jit(solution)/shard_map/ppermute | solution.py:62
  66.2 7.6 %collective-permute-start.16 = (bf16[128,1024]{1,0:T(8,128)(2,1)S(1)}, bf16[128,1024]{1,0:T(8,128)(2,1)S(1)}, u32[]{:S(2)}, u32[]{:S(2)}) collective-permute-start(bf16[128,1024]{1,0:T(8,128)(2,1)S(1)} %fusion.3), channel_id=1, source_target_pairs={{0,32},{1,33},{2,34},{3,35},{4,36},{5,37},{6,38},{7,39},{8,40},{9,... | collective-permute-start | bytes 786440 | tf_op jit(solution)/shard_map/ppermute | solution.py:62
  66.2 13.3 %collective-permute-start.18 = (bf16[512,448]{0,1:T(8,128)(2,1)S(1)}, bf16[512,448]{0,1:T(8,128)(2,1)S(1)}, u32[]{:S(2)}, u32[]{:S(2)}) collective-permute-start(bf16[512,448]{0,1:T(8,128)(2,1)S(1)} %get-tuple-element.74), channel_id=1, source_target_pairs={{0,16},{1,17},{2,18},{3,19},{4,20},{5,21},{6,22},{7,23},{8,24},{9,... | collective-permute-start | bytes 1376264 | tf_op jit(solution)/shard_map/ppermute | solution.py:62
  73.6 7.0 %collective-permute-start.15 = (bf16[128,1024]{1,0:T(8,128)(2,1)S(1)}, bf16[128,1024]{1,0:T(8,128)(2,1)S(1)}, u32[]{:S(2)}, u32[]{:S(2)}) collective-permute-start(bf16[128,1024]{1,0:T(8,128)(2,1)S(1)} %collective-permute-done.14), channel_id=1, source_target_pairs={{0,32},{1,33},{2,34},{3,35},{4,36},{5,37},{6,38},{7,39},{8,40},{9,... | collective-permute-start | bytes 786440 | tf_op jit(solution)/shard_map/ppermute | solution.py:62
  73.8 8.1 %collective-permute-start.17 = (bf16[128,1024]{1,0:T(8,128)(2,1)S(1)}, bf16[128,1024]{1,0:T(8,128)(2,1)S(1)}, u32[]{:S(2)}, u32[]{:S(2)}) collective-permute-start(bf16[128,1024]{1,0:T(8,128)(2,1)S(1)} %collective-permute-done.16), channel_id=1, source_target_pairs={{0,224},{1,225},{2,226},{3,227},{4,228},{5,229},{6,230},{7,231},{8... | collective-permute-start | bytes 786440 | tf_op jit(solution)/shard_map/ppermute | solution.py:62
  81.9 7.6 %collective-permute-start.19 = (bf16[128,1024]{1,0:T(8,128)(2,1)S(1)}, bf16[128,1024]{1,0:T(8,128)(2,1)S(1)}, u32[]{:S(2)}, u32[]{:S(2)}) collective-permute-start(bf16[128,1024]{1,0:T(8,128)(2,1)S(1)} %collective-permute-done.15), channel_id=1, source_target_pairs={{0,224},{1,225},{2,226},{3,227},{4,228},{5,229},{6,230},{7,231},{8... | collective-permute-start | bytes 786440 | tf_op jit(solution)/shard_map/ppermute | solution.py:62
  83.5 7.5 %collective-permute-start.21 = (bf16[128,1024]{1,0:T(8,128)(2,1)S(1)}, bf16[128,1024]{1,0:T(8,128)(2,1)S(1)}, u32[]{:S(2)}, u32[]{:S(2)}) collective-permute-start(bf16[128,1024]{1,0:T(8,128)(2,1)S(1)} %collective-permute-done.17), channel_id=1, source_target_pairs={{0,32},{1,33},{2,34},{3,35},{4,36},{5,37},{6,38},{7,39},{8,40},{9,... | collective-permute-start | bytes 786440 | tf_op jit(solution)/shard_map/ppermute | solution.py:62
  100.7 10.1 %collective-permute-start.30 = (bf16[128,448]{0,1:T(8,128)(2,1)S(1)}, bf16[128,448]{0,1:T(8,128)(2,1)S(1)}, u32[]{:S(2)}, u32[]{:S(2)}) collective-permute-start(bf16[128,448]{0,1:T(8,128)(2,1)S(1)} %get-tuple-element.85), channel_id=1, source_target_pairs={{0,8},{1,9},{2,10},{3,11},{4,12},{5,13},{6,14},{7,15},{8,0},{9,1},... | collective-permute-start | bytes 344072 | tf_op jit(solution)/shard_map/ppermute | solution.py:62
  102.1 8.8 %collective-permute-start.29 = (bf16[128,448]{0,1:T(8,128)(2,1)S(1)}, bf16[128,448]{0,1:T(8,128)(2,1)S(1)}, u32[]{:S(2)}, u32[]{:S(2)}) collective-permute-start(bf16[128,448]{0,1:T(8,128)(2,1)S(1)} %get-tuple-element.86), channel_id=1, source_target_pairs={{0,12},{1,13},{2,14},{3,15},{4,8},{5,9},{6,10},{7,11},{8,4},{9,5},... | collective-permute-start | bytes 344072 | tf_op jit(solution)/shard_map/ppermute | solution.py:62
  104.2 6.6 %collective-permute-start.28 = (bf16[128,448]{0,1:T(8,128)(2,1)S(1)}, bf16[128,448]{0,1:T(8,128)(2,1)S(1)}, u32[]{:S(2)}, u32[]{:S(2)}) collective-permute-start(bf16[128,448]{0,1:T(8,128)(2,1)S(1)} %get-tuple-element.84), channel_id=1, source_target_pairs={{0,4},{1,5},{2,6},{3,7},{4,0},{5,1},{6,2},{7,3},{8,12},{9,13},{10,... | collective-permute-start | bytes 344072 | tf_op jit(solution)/shard_map/ppermute | solution.py:62
  106.1 6.7 %collective-permute-start.26 = (bf16[128,448]{0,1:T(8,128)(2,1)S(1)}, bf16[128,448]{0,1:T(8,128)(2,1)S(1)}, u32[]{:S(2)}, u32[]{:S(2)}) collective-permute-start(bf16[128,448]{0,1:T(8,128)(2,1)S(1)} %get-tuple-element.88), channel_id=1, source_target_pairs={{0,8},{1,9},{2,10},{3,11},{4,12},{5,13},{6,14},{7,15},{8,0},{9,1},... | collective-permute-start | bytes 344072 | tf_op jit(solution)/shard_map/ppermute | solution.py:62
  108.7 6.5 %collective-permute-start.25 = (bf16[128,448]{0,1:T(8,128)(2,1)S(1)}, bf16[128,448]{0,1:T(8,128)(2,1)S(1)}, u32[]{:S(2)}, u32[]{:S(2)}) collective-permute-start(bf16[128,448]{0,1:T(8,128)(2,1)S(1)} %get-tuple-element.89), channel_id=1, source_target_pairs={{0,12},{1,13},{2,14},{3,15},{4,8},{5,9},{6,10},{7,11},{8,4},{9,5},... | collective-permute-start | bytes 344072 | tf_op jit(solution)/shard_map/ppermute | solution.py:62
  120.7 16.3 %collective-permute-start.32 = (bf16[128,448]{0,1:T(8,128)(2,1)S(1)}, bf16[128,448]{0,1:T(8,128)(2,1)S(1)}, u32[]{:S(2)}, u32[]{:S(2)}) collective-permute-start(bf16[128,448]{0,1:T(8,128)(2,1)S(1)} %add_convert_fusion), channel_id=1, source_target_pairs={{0,0},{1,1},{2,32},{3,33},{4,64},{5,65},{6,96},{7,97},{8,128},{9,1... | collective-permute-start | bytes 344072 | tf_op jit(solution)/shard_map/ppermute | solution.py:62
  (21 other events, 95.8 us)
